TPU v7x, 32 devices: a whole 2x2x4 slice. The times are simulated.
32 devices in a mesh: grp: 2 (over x), gx: 16 (over z, y, core).
Axes of the slice: x: 2, y: 2, z: 4, core: 2. Of those that a mesh axis runs over, the one named last changes fastest.
Arguments:
- tensor: float32 [128, 1152, 576], P(('grp', 'gx')), parts along dimension 0, may hold values from -6 to 6
- factor_b: float32 [2304, 256], P('grp'), parts along dimension 0, may hold values from -7 to 7
- factor_c: float32 [1152, 256], P('grp'), parts along dimension 0, may hold values from -7 to 7
Outputs:
- new_a: float32 [128, 256], P(('grp', 'gx')), parts along dimension 0
- new_b: float32 [2304, 256], P(('grp', 'gx')), parts along dimension 0
- new_c: float32 [1152, 256], P(('grp', 'gx')), parts along dimension 0
There are 2 independent parts, one for each index of `grp`. A program takes and returns all parts, laid end to end along the dimension named above; each array names one. Nothing has to cross between parts.
All inputs are finite; a program needn't handle non-finite values.
Results may differ from a plain program's by a relative error of at most 0.0003.
Values sent between devices are 32-bit elements; how exact they have to be, the bound alone decides.
No kernel may reach another device: no remote copies, remote signals or barrier semaphores. Data moves between devices by JAX's collectives and lax.ppermute only.
A program may use at most 64 MiB of HBM per device.

v0:
```python
import jax
import jax.numpy as jnp
from jax import lax
from jax.sharding import PartitionSpec as P


def gram(factor):
    return jnp.dot(
        factor.T, factor, precision=lax.Precision.HIGHEST, preferred_element_type=jnp.float32
    )


def system(first, second):
    product = first * second
    ridge = 0.1 * jnp.mean(jnp.diagonal(product))
    return product + ridge * jnp.eye(product.shape[0], dtype=jnp.float32)


def solve(right, matrix):
    lower = jnp.linalg.cholesky(matrix)
    return jax.scipy.linalg.cho_solve((lower, True), right.T).T


def column_scale(sums, count):
    return jnp.sqrt(count / (sums + 1e-06))


def local(tensor, factor_b, factor_c):
    high = lax.Precision.HIGHEST
    devices = lax.axis_size("gx")
    rows_here = tensor.shape[0]
    total_first = rows_here * devices
    total_second = tensor.shape[1]
    total_third = tensor.shape[2]
    contracted = jnp.einsum("ijk,kr->ijr", tensor, factor_c, precision=high)
    first_side = jnp.einsum("ijr,jr->ir", contracted, factor_b, precision=high)
    gram_c = gram(factor_c)
    raw_a = solve(first_side, system(gram(factor_b), gram_c))
    sums_a = lax.psum(jnp.sum(raw_a * raw_a, axis=0), "gx")
    new_a = raw_a * column_scale(sums_a, total_first)
    gram_a = lax.psum(gram(new_a), "gx")
    system_b = system(gram_a, gram_c)
    block = contracted
    side_b = lax.psum_scatter(
        jnp.einsum("ijr,ir->jr", block, new_a, precision=high),
        "gx",
        scatter_dimension=0,
        tiled=True,
    )
    raw_b = solve(side_b, system_b)
    start_fold = (
        jnp.zeros((rows_here, total_third, raw_b.shape[1]), jnp.float32),
        jnp.zeros((raw_b.shape[1], raw_b.shape[1]), jnp.float32),
    )
    piece = lax.all_gather(raw_b, "gx", axis=0, tiled=True)
    block = tensor
    fold_second = start_fold[0] + jnp.einsum("ijk,jr->ikr", block, piece, precision=high)
    raw_gram_b = gram(piece)
    scale_b = column_scale(jnp.diagonal(raw_gram_b), total_second)
    new_b = raw_b * scale_b
    gram_b = raw_gram_b * scale_b[:, None] * scale_b[None, :]
    second = fold_second * scale_b
    system_c = system(gram_a, gram_b)
    block = second
    side_c = lax.psum_scatter(
        jnp.einsum("ikr,ir->kr", block, new_a, precision=high),
        "gx",
        scatter_dimension=0,
        tiled=True,
    )
    raw_c = solve(side_c, system_c)
    sums_c = lax.psum(jnp.sum(raw_c * raw_c, axis=0), "gx")
    new_c = raw_c * column_scale(sums_c, total_third)
    return (new_a, new_b, new_c)


def solution(mesh):
    placed = (P(("grp", "gx"), None, None), P("grp", None), P("grp", None))
    return jax.shard_map(
        local,
        mesh=mesh,
        in_specs=placed,
        out_specs=(P(("grp", "gx"), None), P(("grp", "gx"), None), P(("grp", "gx"), None)),
        check_vma=False,
    )
```

profile of v0, /device:TPU:0, one launch (start us, length us, event | category | flops | bytes accessed | tf_op | source)
XLA Modules:
  0.0 520.1 jit_solution(12628404989565853324)
XLA Ops:
  9.5 2.1 convolution_multiply_fusion
  11.6 2.6 gather_fusion
  15.7 11.7 %cholesky.172 = f32[128,128]{1,0:T(8,128)S(1)} custom-call(f32[128,128]{1,0:T(8,128)S(1)} %cholesky.270), custom_call_target="Cholesky" | custom-call | tf_op jit(solution)/shard_map/jit(cholesky)/cholesky | solution.py:20
  27.4 9.8 %custom-call.42 = f32[1,128,128]{1,2,0:T(8,128)S(1)} custom-call(f32[1,128,128]{2,1,0:T(8,128)S(1)} %get-tuple-element.99), custom_call_target="InvertDiagBlocksLowerTriangular" | custom-call | tf_op jit(solution)/shard_map/jit(cholesky)/cholesky | solution.py:20
  37.7 11.7 %cholesky.189 = f32[128,128]{1,0:T(8,128)S(1)} custom-call(f32[128,128]{1,0:T(8,128)S(1)} %convolution_subtract_fusion.2), custom_call_target="Cholesky" | custom-call | tf_op jit(solution)/shard_map/jit(cholesky)/cholesky | solution.py:20
  52.0 4.3 while.3
  52.7 1.4 dynamic-slice.22
  54.8 1.4 dynamic-slice.22
  56.4 20.1 %custom-call.29 = f32[2,128,128]{1,2,0:T(8,128)S(1)} custom-call(f32[2,128,128]{2,1,0:T(8,128)S(1)} %get-tuple-element.11), custom_call_target="InvertDiagBlocksLowerTriangular" | custom-call | tf_op jit(solution)/shard_map/jit(_cho_solve)/triangular_solve | solution.py:21
  76.5 22.4 %multiply_reduce_fusion.1 = (f32[256,4]{0,1:T(4,128)S(1)}, f32[4,1152,256]{2,1,0:T(8,128)}) fusion(f32[256,1152]{0,1:T(8,128)S(1)} %bitcast.153, f32[4,1152,576]{1,2,0:T(8,128)} %param.4, f32[576,256]{1,0:T(8,128)S(1)} %copy-done), kind=kOutput, calls=%fused_computation.11 | convolution fusion | flops 8156085248 | bytes 17108992 | tf_op jit(solution)/shard_map/ijk,kr->ijr/dot_general | solution.py:35
  100.1 34.9 %psum.21 = f32[256]{0:T(256)S(1)} all-reduce(f32[256]{0:T(256)S(1)} %multiply_reduce_fusion.4), channel_id=1, replica_groups=mesh['grp'=2,'gx'=16] {'gx'}, use_global_device_ids=true, to_apply=%region_6.8 | all-reduce | flops 256 | bytes 2048 | tf_op jit(solution)/shard_map/psum | solution.py:39
  136.3 3.9 multiply_reduce_fusion
  140.2 82.2 %all-reduce.5.cloned.1.call-done = f32[256,256]{0,1:T(8,128)} async-done(((f32[256,256]{0,1:T(8,128)}), f32[256,256]{0,1:T(8,128)}) %all-reduce.5.cloned.1.call-update) | async-done | bytes 262160 | tf_op jit(solution)/shard_map/psum | solution.py:41
  223.4 2.5 gather_fusion.1
  227.4 11.7 %cholesky.206 = f32[128,128]{1,0:T(8,128)S(1)} custom-call(f32[128,128]{1,0:T(8,128)S(1)} %cholesky.273), custom_call_target="Cholesky" | custom-call | tf_op jit(solution)/shard_map/jit(cholesky)/cholesky | solution.py:20
  239.2 9.8 %custom-call.43 = f32[1,128,128]{1,2,0:T(8,128)S(1)} custom-call(f32[1,128,128]{2,1,0:T(8,128)S(1)} %get-tuple-element.97), custom_call_target="InvertDiagBlocksLowerTriangular" | custom-call | tf_op jit(solution)/shard_map/jit(cholesky)/cholesky | solution.py:20
  249.7 11.7 %cholesky.223 = f32[128,128]{1,0:T(8,128)S(1)} custom-call(f32[128,128]{1,0:T(8,128)S(1)} %convolution_subtract_fusion.1), custom_call_target="Cholesky" | custom-call | tf_op jit(solution)/shard_map/jit(cholesky)/cholesky | solution.py:20
  264.1 4.0 while.4
  268.1 19.7 %custom-call.30 = f32[2,128,128]{1,2,0:T(8,128)S(1)} custom-call(f32[2,128,128]{2,1,0:T(8,128)S(1)} %get-tuple-element.19), custom_call_target="InvertDiagBlocksLowerTriangular" | custom-call | tf_op jit(solution)/shard_map/jit(_cho_solve)/triangular_solve | solution.py:21
  292.9 37.6 %all-gather.2.cloned.1.call-done = f32[1152,256]{1,0:T(8,128)} async-done(((f32[72,256]{1,0:T(8,128)}), f32[1152,256]{1,0:T(8,128)}) %all-gather.2.cloned.1.call-update) | async-done | bytes 1179664 | tf_op jit(solution)/shard_map/all_gather | solution.py:55
  330.5 3.7 fusion.42
  334.2 2.6 gather_fusion.2
  337.0 2.4 gather_fusion.3
  340.9 11.7 %cholesky.240 = f32[128,128]{1,0:T(8,128)S(1)} custom-call(f32[128,128]{1,0:T(8,128)S(1)} %cholesky.276), custom_call_target="Cholesky" | custom-call | tf_op jit(solution)/shard_map/jit(cholesky)/cholesky | solution.py:20
  352.6 9.8 %custom-call.44 = f32[1,128,128]{1,2,0:T(8,128)S(1)} custom-call(f32[1,128,128]{2,1,0:T(8,128)S(1)} %get-tuple-element.95), custom_call_target="InvertDiagBlocksLowerTriangular" | custom-call | tf_op jit(solution)/shard_map/jit(cholesky)/cholesky | solution.py:20
  362.9 11.7 %cholesky.257 = f32[128,128]{1,0:T(8,128)S(1)} custom-call(f32[128,128]{1,0:T(8,128)S(1)} %convolution_subtract_fusion), custom_call_target="Cholesky" | custom-call | tf_op jit(solution)/shard_map/jit(cholesky)/cholesky | solution.py:20
  375.0 12.2 %multiply_reduce_fusion.2 = f32[256,576]{0,1:T(8,128)S(1)} fusion(f32[4,1152,576]{1,2,0:T(8,128)} %param.4, f32[256,4]{0,1:T(4,128)S(1)} %fusion.35, f32[1152,256]{1,0:T(8,128)S(1)} %copy-done.2, f32[256]{0:T(256)S(1)} %divide_sqrt_fusion.1), kind=kOutput, calls=%fused_computation.12 | convolution fusion | flops 8155348992 | bytes 12391424 | tf_op jit(solution)/shard_map/ijk,jr->ikr/dot_general | solution.py:57
  391.0 4.2 while.5
  391.6 1.4 dynamic-slice.26
  395.2 19.7 %custom-call.31 = f32[2,128,128]{1,2,0:T(8,128)S(1)} custom-call(f32[2,128,128]{2,1,0:T(8,128)S(1)} %get-tuple-element.27), custom_call_target="InvertDiagBlocksLowerTriangular" | custom-call | tf_op jit(solution)/shard_map/jit(_cho_solve)/triangular_solve | solution.py:21
  415.5 63.2 %all-reduce.7.cloned.1.call-done = f32[576,256]{0,1:T(8,128)} async-done(((f32[576,256]{0,1:T(8,128)}), f32[576,256]{0,1:T(8,128)}) %all-reduce.7.cloned.1.call-update) | async-done | bytes 589840
  481.2 31.2 %psum.23 = f32[256]{0:T(256)S(1)} all-reduce(f32[256]{0:T(256)S(1)} %multiply_reduce_fusion.3), channel_id=1, replica_groups=mesh['grp'=2,'gx'=16] {'gx'}, use_global_device_ids=true, to_apply=%region_13.15 | all-reduce | flops 256 | bytes 2048 | tf_op jit(solution)/shard_map/psum | solution.py:72
  (143 shorter events, 31.7 us)
Async XLA Ops:
  7.2 1.1 copy-start
  7.2 2.3 copy-start.1
  7.2 215.2 %all-reduce.5.cloned.1.call-start = ((), (), s32[]{:S(2)}) async-start(), calls=%async_computation.1 | async-start | bytes 524288 | tf_op jit(solution)/shard_map/psum | solution.py:41
  135.1 239.9 %copy-start.4 = (f32[256,4]{0,1:T(4,128)}, f32[256,4]{0,1:T(4,128)S(1)}, u32[]{:S(2)}) copy-start(f32[256,4]{0,1:T(4,128)S(1)} %fusion.35) | copy-start | bytes 12292
  136.2 151.6 %reduce-scatter.5.cloned.1.call-start = ((), (), s32[]{:S(2)}) async-start(), calls=%async_computation.3 | async-start | bytes 1253376 | tf_op jit(solution)/shard_map/reduce_scatter | solution.py:44
  140.2 190.3 %all-gather.2.cloned.1.call-start = ((), (), s32[]{:S(2)}) async-start(), calls=%async_computation.2 | async-start | bytes 1253376 | tf_op jit(solution)/shard_map/all_gather | solution.py:55
  261.4 30.2 %copy-start.5 = (u32[32]{0:T(128)S(1)}, u32[32]{0:T(128)}, u32[]{:S(2)}) copy-start(u32[32]{0:T(128)} %constant.240) | copy-start | bytes 388
  290.6 46.3 %copy-start.3 = (f32[256,256]{0,1:T(8,128)S(1)}, f32[256,256]{0,1:T(8,128)}, u32[]{:S(2)}) copy-start(f32[256,256]{0,1:T(8,128)} %all-reduce.5.cloned.1.call-done) | copy-start | bytes 786436
  291.5 187.2 %all-reduce.7.cloned.1.call-start = ((), (), s32[]{:S(2)}) async-start(), calls=%async_computation.4 | async-start | bytes 1310720
  336.9 38.1 %copy-start.2 = (f32[1152,256]{1,0:T(8,128)S(1)}, f32[1152,256]{1,0:T(8,128)}, u32[]{:S(2)}) copy-start(f32[1152,256]{1,0:T(8,128)} %all-gather.2.cloned.1.call-done) | copy-start | bytes 3538948
Sparse Core Ops, SparseCore 0:
  136.4 86.0 all-reduce.4
  226.0 58.9 reduce-scatter.4
  291.6 38.8 all-gather.1
  388.4 90.2 all-reduce.6
where the time goes:
time: 524 us; the launch traced here: 520 us
  waiting for transfers between devices  183 us (35%)
  other arithmetic  172 us (33%)
  blocking collectives  66.1 us (13%)
  matrix products  49.5 us (9%)
  local copies, waits for them, and re-layouts  27.8 us (5%)
  between operations  21.2 us (4%)
    another operation x20, other arithmetic, solve(): lower = jnp.linalg.cholesky(matrix)  103 us
    psum x1, waiting for transfers between devices, local(): gram_a = lax.psum(gram(new_a), 'gx')  82.2 us
    unnamed x5, waiting for transfers between devices  63.3 us
    another operation x7, other arithmetic, solve(): return jax.scipy.linalg.cho_solve((lower, True), right.T).T  59.6 us
    all_gather x1, waiting for transfers between devices, local(): piece = lax.all_gather(raw_b, 'gx', axis=0, tiled=True)  37.6 us
    psum x1, blocking collectives, local(): sums_a = lax.psum(jnp.sum(raw_a * raw_a, axis=0), 'gx')  34.9 us
    psum x1, blocking collectives, local(): sums_c = lax.psum(jnp.sum(raw_c * raw_c, axis=0), 'gx')  31.2 us
    dot_general x1, matrix products, local(): contracted = jnp.einsum('ijk,kr->ijr', tensor, factor_c, precision=high)  22.4 us
  transfers between devices with their start and end apart: 4, of which 3 were waited for; matrix products, arithmetic and copies ran while one was open for 18% of the time, Pallas kernels for 0%

commit v1 on v0

v1 whole, which is shorter than its diff:
```python
import functools

import jax
import jax.numpy as jnp
from jax import lax
from jax.experimental import pallas as pl
from jax.experimental.pallas import tpu as pltpu
from jax.sharding import PartitionSpec as P

HIGH = lax.Precision.HIGHEST
PANEL = 32
LIMIT = 56 * 1024 * 1024


def dot(a, b):
    return jnp.dot(a, b, precision=HIGH, preferred_element_type=jnp.float32)


def dot_first(a, b):
    return lax.dot_general(
        a, b, (((0,), (0,)), ((), ())), precision=HIGH, preferred_element_type=jnp.float32
    )


def split(x):
    high = x.astype(jnp.bfloat16)
    low = (x - high.astype(jnp.float32)).astype(jnp.bfloat16)
    return high, low


def mul(a, b):
    return jnp.dot(a, b, preferred_element_type=jnp.float32)


def eye_mask(size):
    return lax.broadcasted_iota(jnp.int32, (size, size), 0) == lax.broadcasted_iota(
        jnp.int32, (size, size), 1
    )


def system(first, second):
    size = first.shape[0]
    product = first * second
    diagonal = jnp.where(eye_mask(size), product, 0.0)
    ridge = 0.1 * (jnp.sum(diagonal) / size)
    return product + jnp.where(eye_mask(size), ridge, 0.0)


def eliminate(ref, first, last):
    size = ref.shape[0]
    tiles = size // 128
    groups = PANEL // 8
    lane = lax.broadcasted_iota(jnp.int32, (8, 128), 1)
    sub = lax.broadcasted_iota(jnp.int32, (8, 128), 0)
    for panel in range(first, last):
        start = panel * PANEL
        rows = [
            [ref[start + 8 * t : start + 8 * t + 8, 128 * h : 128 * h + 128] for h in range(tiles)]
            for t in range(groups)
        ]
        for q in range(groups):
            column = start + 8 * q
            home, offset = column // 128, column % 128
            cols = [
                [
                    jnp.broadcast_to(rows[t][home][:, offset + k : offset + k + 1], (8, 128))
                    for k in range(8)
                ]
                for t in range(groups)
            ]
            for k in range(8):
                inverse = 1.0 / cols[q][k][k : k + 1, :]
                here = lane == offset + k
                pivot = sub == k
                for j in range(k + 1, 8):
                    scaled = cols[q][j][k : k + 1, :] * inverse
                    for t in range(groups):
                        fresh = cols[t][j] - cols[t][k] * scaled
                        if t == q:
                            fresh = jnp.where(pivot, scaled, fresh)
                        cols[t][j] = fresh
                for h in range(tiles):
                    row = rows[q][h][k : k + 1, :]
                    if h == home:
                        row = jnp.where(here[:1], 1.0, row)
                    row = row * inverse
                    for t in range(groups):
                        base = rows[t][h]
                        if h == home:
                            base = jnp.where(here, 0.0, base)
                        fresh = base - cols[t][k] * row
                        if t == q:
                            fresh = jnp.where(pivot, row, fresh)
                        rows[t][h] = fresh
        home, offset = start // 128, start % 128
        solved = jnp.concatenate([jnp.concatenate(group, axis=1) for group in rows], axis=0)
        parts = [solved]
        if offset:
            parts.insert(0, jnp.zeros((offset, size), jnp.float32))
        if offset + PANEL < 128:
            parts.append(jnp.zeros((128 - offset - PANEL, size), jnp.float32))
        left = ref[:, 128 * home : 128 * home + 128]
        wide = lax.broadcasted_iota(jnp.int32, (size, 128), 1)
        inside = (wide >= offset) & (wide < offset + PANEL)
        change = dot(left, jnp.concatenate(parts, axis=0))
        for h in range(tiles):
            base = ref[:, 128 * h : 128 * h + 128]
            if h == home:
                base = jnp.where(inside, 0.0, base)
            ref[:, 128 * h : 128 * h + 128] = base - change[:, 128 * h : 128 * h + 128]
        ref[start : start + PANEL, :] = solved


def invert(ref):
    eliminate(ref, 0, ref.shape[0] // PANEL)


def first_kernel(x_ref, b_ref, c_ref, raw_ref, side_ref, gram_ref, inv, turned, halves, out, cast):
    i = pl.program_id(0)
    count = pl.num_programs(0)

    @pl.when(i == 0)
    def _():
        c = c_ref[...]
        gram_c = dot_first(c, c)
        gram_ref[...] = gram_c
        b = b_ref[...]
        inv[...] = system(dot_first(b, b), gram_c)
        invert(inv)
        turned[...] = b.T
        high, low = split(c.T)
        halves[0] = high
        halves[1] = low
        cast[...] = jnp.zeros_like(cast)

    high, low = split(x_ref[0])
    block = mul(halves[0], high) + mul(halves[0], low) + mul(halves[1], high)
    out[i] = block
    sums = jnp.sum(block * turned[...], axis=1, keepdims=True)
    lane = lax.broadcasted_iota(jnp.int32, cast.shape, 1)
    cast[...] = jnp.where(lane == i, sums, cast[...])

    @pl.when(i == count - 1)
    def _():
        raw = dot(inv[...], cast[...])
        total = out[0] * raw[:, 0:1]
        for n in range(1, out.shape[0]):
            total = total + out[n] * raw[:, n : n + 1]
        side_ref[...] = total
        raw_ref[...] = raw.T[: raw_ref.shape[0], :]


def first_call(turned, factor_b, factor_c):
    count, depth, width = turned.shape
    rank = factor_b.shape[1]
    whole = lambda i: (0, 0)
    return pl.pallas_call(
        first_kernel,
        grid=(count,),
        in_specs=[
            pl.BlockSpec((1, depth, width), lambda i: (i, 0, 0)),
            pl.BlockSpec((width, rank), whole),
            pl.BlockSpec((depth, rank), whole),
        ],
        out_specs=[
            pl.BlockSpec((count, rank), whole),
            pl.BlockSpec((rank, width), whole),
            pl.BlockSpec((rank, rank), whole),
        ],
        out_shape=[
            jax.ShapeDtypeStruct((count, rank), jnp.float32),
            jax.ShapeDtypeStruct((rank, width), jnp.float32),
            jax.ShapeDtypeStruct((rank, rank), jnp.float32),
        ],
        scratch_shapes=[
            pltpu.VMEM((rank, rank), jnp.float32),
            pltpu.VMEM((rank, width), jnp.float32),
            pltpu.VMEM((2, rank, depth), jnp.bfloat16),
            pltpu.VMEM((count, rank, width), jnp.float32),
            pltpu.VMEM((rank, 128), jnp.float32),
        ],
        compiler_params=pltpu.CompilerParams(vmem_limit_bytes=LIMIT),
        cost_estimate=pl.CostEstimate(
            flops=6 * count * depth * width * rank, bytes_accessed=turned.size * 4, transcendentals=0
        ),
    )(turned, factor_b, factor_c)


def scales(gram, count):
    diagonal = jnp.where(eye_mask(gram.shape[0]), gram, 0.0)
    row = jnp.sqrt(count / (jnp.sum(diagonal, axis=0, keepdims=True) + 1e-06))
    column = jnp.sqrt(count / (jnp.sum(diagonal, axis=1, keepdims=True) + 1e-06))
    return row, column


def second_kernel(count, all_ref, own_ref, gram_c_ref, new_ref, gram_ref, inv_ref, work):
    rows = all_ref[...]
    raw = dot_first(rows, rows)
    row, column = scales(raw, count)
    gram = raw * row * column
    gram_ref[...] = gram
    new_ref[...] = own_ref[...] * row
    work[...] = system(gram, gram_c_ref[...])
    invert(work)
    inv_ref[...] = work[...] * column


def second_call(gathered, own, gram_c):
    rank = own.shape[1]
    square = jax.ShapeDtypeStruct((rank, rank), jnp.float32)
    return pl.pallas_call(
        functools.partial(second_kernel, float(gathered.shape[0])),
        out_shape=[jax.ShapeDtypeStruct(own.shape, jnp.float32), square, square],
        scratch_shapes=[pltpu.VMEM((rank, rank), jnp.float32)],
        compiler_params=pltpu.CompilerParams(vmem_limit_bytes=LIMIT),
        cost_estimate=pl.CostEstimate(flops=10**10, bytes_accessed=10**6, transcendentals=0),
    )(gathered, own, gram_c)


def third_kernel(x_ref, a_ref, side_ref, inv_ref, raw_ref, new_ref, gram_ref, out_ref, halves, total):
    i = pl.program_id(0)
    count = pl.num_programs(0)
    width = x_ref.shape[2]

    @pl.when(i == 0)
    def _():
        raw = dot(side_ref[...].T, inv_ref[...])
        high, low = split(raw)
        halves[0] = high
        halves[1] = low
        gram = dot_first(raw, raw)
        row, column = scales(gram, float(width))
        raw_ref[...] = raw * row
        gram_ref[...] = gram * row * column
        new_ref[...] = row
        total[...] = jnp.zeros_like(total)

    high, low = split(x_ref[0])
    block = mul(high, halves[0]) + mul(low, halves[0]) + mul(high, halves[1])
    total[...] += block * a_ref[pl.ds(i, 1), :]

    @pl.when(i == count - 1)
    def _():
        result = total[...] * new_ref[...]
        devices, padded, _ = out_ref.shape
        rows = result.shape[0] // devices
        steps = devices.bit_length() - 1
        for d in range(devices):
            place = sum(((d >> b) & 1) << (steps - 1 - b) for b in range(steps))
            out_ref[place, :rows, :] = result[d * rows : (d + 1) * rows, :]
            if padded > rows:
                out_ref[place, rows:, :] = jnp.zeros((padded - rows, result.shape[1]), jnp.float32)


def third_call(turned, new_a, side, inv, devices):
    count, depth, width = turned.shape
    rank = new_a.shape[1]
    padded = -(-(depth // devices) // 8) * 8
    whole = lambda i: (0, 0)
    return pl.pallas_call(
        third_kernel,
        grid=(count,),
        in_specs=[
            pl.BlockSpec((1, depth, width), lambda i: (i, 0, 0)),
            pl.BlockSpec((count, rank), whole),
            pl.BlockSpec((rank, width), whole),
            pl.BlockSpec((rank, rank), whole),
        ],
        out_specs=[
            pl.BlockSpec((width, rank), whole),
            pl.BlockSpec((1, rank), whole),
            pl.BlockSpec((rank, rank), whole),
            pl.BlockSpec((devices, padded, rank), lambda i: (0, 0, 0)),
        ],
        out_shape=[
            jax.ShapeDtypeStruct((width, rank), jnp.float32),
            jax.ShapeDtypeStruct((1, rank), jnp.float32),
            jax.ShapeDtypeStruct((rank, rank), jnp.float32),
            jax.ShapeDtypeStruct((devices, padded, rank), jnp.float32),
        ],
        scratch_shapes=[
            pltpu.VMEM((2, width, rank), jnp.bfloat16),
            pltpu.VMEM((depth, rank), jnp.float32),
        ],
        compiler_params=pltpu.CompilerParams(vmem_limit_bytes=LIMIT),
        cost_estimate=pl.CostEstimate(
            flops=6 * count * depth * width * rank, bytes_accessed=turned.size * 4, transcendentals=0
        ),
    )(turned, new_a, side, inv)


def fourth_kernel(a_ref, b_ref, out_ref):
    out_ref[...] = system(a_ref[...], b_ref[...])
    invert(out_ref)


def fourth_call(gram_a, gram_b):
    return pl.pallas_call(
        fourth_kernel,
        out_shape=jax.ShapeDtypeStruct(gram_a.shape, jnp.float32),
        compiler_params=pltpu.CompilerParams(vmem_limit_bytes=LIMIT),
        cost_estimate=pl.CostEstimate(flops=10**10, bytes_accessed=10**6, transcendentals=0),
    )(gram_a, gram_b)


def swap(x, bit):
    devices = lax.axis_size("gx")
    return lax.ppermute(x, "gx", [(i, i ^ (1 << bit)) for i in range(devices)])


def scatter(x, steps):
    me = lax.axis_index("gx")
    for bit in range(steps):
        mine = (me >> bit) & 1
        half = x.shape[0] // 2
        x = x.reshape((2, half) + x.shape[1:])
        keep = lax.dynamic_index_in_dim(x, mine, 0, keepdims=False)
        send = lax.dynamic_index_in_dim(x, 1 - mine, 0, keepdims=False)
        x = keep + swap(send, bit)
    return x


def gather(x, steps):
    me = lax.axis_index("gx")
    for bit in reversed(range(steps)):
        mine = (me >> bit) & 1
        other = swap(x, bit)
        x = jnp.where(
            mine == 0, jnp.concatenate([x, other], axis=0), jnp.concatenate([other, x], axis=0)
        )
    return x


def local(tensor, factor_b, factor_c):
    devices = lax.axis_size("gx")
    me = lax.axis_index("gx")
    steps = devices.bit_length() - 1
    total_second, total_third = tensor.shape[1], tensor.shape[2]
    turned = jnp.swapaxes(tensor, 1, 2)
    raw_a, side_b, gram_c = first_call(turned, factor_b, factor_c)
    gathered = raw_a
    for bit in range(steps):
        gathered = jnp.concatenate([gathered, swap(gathered, bit)], axis=0)
    rank = raw_a.shape[1]
    side_b = side_b.reshape(devices, rank // devices, total_second)
    side_b = gather(scatter(side_b, steps), steps).reshape(rank, total_second)
    new_a, gram_a, inv_b = second_call(gathered, raw_a, gram_c)
    all_b, _, gram_b, side_c = third_call(turned, new_a, side_b, inv_b, devices)
    rows_b = total_second // devices
    new_b = lax.dynamic_slice_in_dim(all_b, me * rows_b, rows_b, axis=0)
    inv_c = fourth_call(gram_a, gram_b)
    side_c = scatter(side_c, steps)[0]
    raw_c = dot(side_c, inv_c)[: total_third // devices]
    sums = jnp.sum(raw_c * raw_c, axis=0, keepdims=True)
    for bit in range(steps):
        sums = sums + swap(sums, bit)
    new_c = raw_c * jnp.sqrt(total_third / (sums + 1e-06))
    return (new_a, new_b, new_c)


def solution(mesh):
    placed = (P(("grp", "gx"), None, None), P("grp", None), P("grp", None))
    return jax.shard_map(
        local,
        mesh=mesh,
        in_specs=placed,
        out_specs=(P(("grp", "gx"), None), P(("grp", "gx"), None), P(("grp", "gx"), None)),
        check_vma=False,
    )
```

time: 524 us -> 151 us (0.29)
  other arithmetic: 172 us -> 3.04 us
  waiting for transfers between devices: 183 us -> 45.6 us
  blocking collectives: 66.1 us -> 0 us
  Pallas kernels: 0 us -> 61.7 us
  matrix products: 49.5 us -> 1.2 us
  starting transfers between devices: 0.16 us -> 31.7 us
  local copies, waits for them, and re-layouts: 27.8 us -> 6.27 us
  between operations: 21.2 us -> 0.79 us
    another operation x27 -> x0, other arithmetic: 163 us -> none  [the longest x20 103 us: solve(): lower = jnp.linalg.cholesky(matrix)]
    psum x1 -> x0, waiting for transfers between devices: 82.2 us -> none  [local(): gram_a = lax.psum(gram(new_a), 'gx')]
    psum x2 -> x0, blocking collectives: 66.1 us -> none  [the longest x1 34.9 us: local(): sums_a = lax.psum(jnp.sum(raw_a * raw_a, axis=0), 'gx')]
    unnamed x5 -> x0, waiting for transfers between devices: 63.3 us -> none
    pallas_call x0 -> x4, Pallas kernels: none -> 61.7 us  [the longest x1 23.7 us: first_call(): pl.pallas_call(first_kernel, grid=(count,), in_specs=[pl.BlockSpec((1, de...]
    ppermute x0 -> x20, waiting for transfers between devices: none -> 45.6 us  [swap(): return lax.ppermute(x, 'gx', [(i, i ^ 1 << bit) for i in range(devices)])]
    dot_general x6 -> x1, matrix products: 42.7 us -> 1.2 us  [dot(): return jnp.dot(a, b, precision=HIGH, preferred_element_type=jnp.float32)]
    all_gather x1 -> x0, waiting for transfers between devices: 37.6 us -> none  [local(): piece = lax.all_gather(raw_b, 'gx', axis=0, tiled=True)]
  transfers between devices with their start and end apart: 4 -> 20, of which waited for: 3 -> 16; matrix products, arithmetic and copies ran while one was open for 18% -> 3% of each run, Pallas kernels for 0% -> 16%
where the time goes in v1:
time: 151 us; the launch traced here: 150 us
  Pallas kernels  61.7 us (41%)
  waiting for transfers between devices  45.6 us (30%)
  starting transfers between devices  31.7 us (21%)
  local copies, waits for them, and re-layouts  6.27 us (4%)
  other arithmetic  3.04 us (2%)
    ppermute x20, waiting for transfers between devices, swap(): return lax.ppermute(x, 'gx', [(i, i ^ 1 << bit) for i in range(devices)])  45.6 us
    ppermute x20, starting transfers between devices, swap(): return lax.ppermute(x, 'gx', [(i, i ^ 1 << bit) for i in range(devices)])  31.7 us
    pallas_call x1, Pallas kernels, first_call(): pl.pallas_call(first_kernel, grid=(count,), in_specs=[pl.BlockSpec((1, de...  23.7 us
    pallas_call x1, Pallas kernels, third_call(): pl.pallas_call(third_kernel, grid=(count,), in_specs=[pl.BlockSpec((1, de...  13.4 us
    pallas_call x1, Pallas kernels, second_call(): pl.pallas_call(functools.partial(second_kernel, float(gathered.shape[0]))...  12.6 us
    pallas_call x1, Pallas kernels, fourth_call(): pl.pallas_call(fourth_kernel, out_shape=jax.ShapeDtypeStruct(gram_a.shape...  12.1 us
  transfers between devices with their start and end apart: 20, of which 16 were waited for; matrix products, arithmetic and copies ran while one was open for 3% of the time, Pallas kernels for 16%

profile of v1, /device:TPU:0, one launch (start us, length us, event | category | flops | bytes accessed | tf_op | source)
XLA Modules:
  0.0 150.3 jit_solution(8470750230758004161)
XLA Ops:
  0.6 23.7 %shard_map.58 = (f32[4,256]{1,0:T(4,128)}, f32[256,1152]{1,0:T(8,128)}, f32[256,256]{1,0:T(8,128)}) custom-call(f32[4,576,1152]{2,1,0:T(8,128)} %bitcast.53, f32[1152,256]{1,0:T(8,128)} %b_ref.1, f32[576,256]{1,0:T(8,128)} %c_ref.1), custom_call_target="tpu_custom_call" | custom-call | flops 4076863488 | bytes 10616832 | tf_op jit(solution)/shard_map/pallas_call | solution.py:157
  26.0 1.6 %collective-permute-done.4 = f32[8,16,1152]{2,1,0:T(8,128)S(1)} collective-permute-done((f32[8,16,1152]{2,1,0:T(8,128)S(1)}, f32[8,16,1152]{2,1,0:T(8,128)S(1)}, u32[]{:S(2)}, u32[]{:S(2)}) %collective-permute-start.4) | collective-permute-done | bytes 589856 | tf_op jit(solution)/shard_map/ppermute | solution.py:308
  27.8 3.0 %collective-permute-start.5 = (f32[4,16,1152]{2,1,0:T(8,128)S(1)}, f32[4,16,1152]{2,1,0:T(8,128)S(1)}, u32[]{:S(2)}, u32[]{:S(2)}) collective-permute-start(f32[4,16,1152]{2,1,0:T(8,128)S(1)} %dynamic-slice_bitcast_fusion.2), channel_id=1, source_target_pairs={{0,2},{1,3},{2,0},{3,1},{4,6},{5,7},{6,4},{7,5},{8,10},{9,11},{10,... | collective-permute-start | bytes 884744 | tf_op jit(solution)/shard_map/ppermute | solution.py:308
  30.7 7.3 %collective-permute-done.5 = f32[4,16,1152]{2,1,0:T(8,128)S(1)} collective-permute-done((f32[4,16,1152]{2,1,0:T(8,128)S(1)}, f32[4,16,1152]{2,1,0:T(8,128)S(1)}, u32[]{:S(2)}, u32[]{:S(2)}) %collective-permute-start.5) | collective-permute-done | bytes 294944 | tf_op jit(solution)/shard_map/ppermute | solution.py:308
  38.1 1.9 %collective-permute-start.6 = (f32[2,16,1152]{2,1,0:T(8,128)S(1)}, f32[2,16,1152]{2,1,0:T(8,128)S(1)}, u32[]{:S(2)}, u32[]{:S(2)}) collective-permute-start(f32[2,16,1152]{2,1,0:T(8,128)S(1)} %dynamic-slice_bitcast_fusion.4), channel_id=1, source_target_pairs={{0,4},{1,5},{2,6},{3,7},{4,0},{5,1},{6,2},{7,3},{8,12},{9,13},{10,... | collective-permute-start | bytes 442376 | tf_op jit(solution)/shard_map/ppermute | solution.py:308
  39.9 3.6 %collective-permute-done.6 = f32[2,16,1152]{2,1,0:T(8,128)S(1)} collective-permute-done((f32[2,16,1152]{2,1,0:T(8,128)S(1)}, f32[2,16,1152]{2,1,0:T(8,128)S(1)}, u32[]{:S(2)}, u32[]{:S(2)}) %collective-permute-start.6) | collective-permute-done | bytes 147488 | tf_op jit(solution)/shard_map/ppermute | solution.py:308
  43.6 2.6 %collective-permute-start.7 = (f32[1,16,1152]{2,1,0:T(8,128)S(1)}, f32[1,16,1152]{2,1,0:T(8,128)S(1)}, u32[]{:S(2)}, u32[]{:S(2)}) collective-permute-start(f32[1,16,1152]{2,1,0:T(8,128)S(1)} %constant_dynamic-slice_fusion.2), channel_id=1, source_target_pairs={{0,8},{1,9},{2,10},{3,11},{4,12},{5,13},{6,14},{7,15},{8,0},{9,1},... | collective-permute-start | bytes 221192 | tf_op jit(solution)/shard_map/ppermute | solution.py:308
  46.2 2.7 %collective-permute-done.7 = f32[1,16,1152]{2,1,0:T(8,128)S(1)} collective-permute-done((f32[1,16,1152]{2,1,0:T(8,128)S(1)}, f32[1,16,1152]{2,1,0:T(8,128)S(1)}, u32[]{:S(2)}, u32[]{:S(2)}) %collective-permute-start.7) | collective-permute-done | bytes 73760 | tf_op jit(solution)/shard_map/ppermute | solution.py:308
  48.9 2.7 %collective-permute-start.8 = (f32[1,16,1152]{2,1,0:T(8,128)S(1)}, f32[1,16,1152]{2,1,0:T(8,128)S(1)}, u32[]{:S(2)}, u32[]{:S(2)}) collective-permute-start(f32[1,16,1152]{2,1,0:T(8,128)S(1)} %dynamic-slice_add_fusion), channel_id=1, source_target_pairs={{0,8},{1,9},{2,10},{3,11},{4,12},{5,13},{6,14},{7,15},{8,0},{9,1},... | collective-permute-start | bytes 221192 | tf_op jit(solution)/shard_map/ppermute | solution.py:308
  51.6 2.6 %collective-permute-done.8 = f32[1,16,1152]{2,1,0:T(8,128)S(1)} collective-permute-done((f32[1,16,1152]{2,1,0:T(8,128)S(1)}, f32[1,16,1152]{2,1,0:T(8,128)S(1)}, u32[]{:S(2)}, u32[]{:S(2)}) %collective-permute-start.8) | collective-permute-done | bytes 73760 | tf_op jit(solution)/shard_map/ppermute | solution.py:308
  54.3 3.5 %collective-permute-start.9 = (f32[2,16,1152]{2,1,0:T(8,128)S(1)}, f32[2,16,1152]{2,1,0:T(8,128)S(1)}, u32[]{:S(2)}, u32[]{:S(2)}) collective-permute-start(f32[2,16,1152]{2,1,0:T(8,128)S(1)} %maximum_select_fusion.3), channel_id=1, source_target_pairs={{0,4},{1,5},{2,6},{3,7},{4,0},{5,1},{6,2},{7,3},{8,12},{9,13},{10,... | collective-permute-start | bytes 442376 | tf_op jit(solution)/shard_map/ppermute | solution.py:308
  57.8 3.1 %collective-permute-done.9 = f32[2,16,1152]{2,1,0:T(8,128)S(1)} collective-permute-done((f32[2,16,1152]{2,1,0:T(8,128)S(1)}, f32[2,16,1152]{2,1,0:T(8,128)S(1)}, u32[]{:S(2)}, u32[]{:S(2)}) %collective-permute-start.9) | collective-permute-done | bytes 147488 | tf_op jit(solution)/shard_map/ppermute | solution.py:308
  60.9 1.6 %collective-permute-start.10 = (f32[4,16,1152]{2,1,0:T(8,128)S(1)}, f32[4,16,1152]{2,1,0:T(8,128)S(1)}, u32[]{:S(2)}, u32[]{:S(2)}) collective-permute-start(f32[4,16,1152]{2,1,0:T(8,128)S(1)} %maximum_select_fusion.2), channel_id=1, source_target_pairs={{0,2},{1,3},{2,0},{3,1},{4,6},{5,7},{6,4},{7,5},{8,10},{9,11},{10,... | collective-permute-start | bytes 884744 | tf_op jit(solution)/shard_map/ppermute | solution.py:308
  63.1 4.7 %collective-permute-done.1 = f32[8,256]{1,0:T(8,128)S(1)} collective-permute-done((f32[8,256]{1,0:T(8,128)S(1)}, f32[8,256]{1,0:T(8,128)S(1)}, u32[]{:S(2)}, u32[]{:S(2)}) %collective-permute-start.1) | collective-permute-done | bytes 8224 | tf_op jit(solution)/shard_map/ppermute | solution.py:308
  67.8 2.1 %collective-permute-start.2 = (f32[16,256]{1,0:T(8,128)S(1)}, f32[16,256]{1,0:T(8,128)S(1)}, u32[]{:S(2)}, u32[]{:S(2)}) collective-permute-start(f32[16,256]{1,0:T(8,128)S(1)} %pad_maximum_fusion.1), channel_id=1, source_target_pairs={{0,4},{1,5},{2,6},{3,7},{4,0},{5,1},{6,2},{7,3},{8,12},{9,13},{10,... | collective-permute-start | bytes 49160 | tf_op jit(solution)/shard_map/ppermute | solution.py:308
  69.9 1.7 %collective-permute-done.2 = f32[16,256]{1,0:T(8,128)S(1)} collective-permute-done((f32[16,256]{1,0:T(8,128)S(1)}, f32[16,256]{1,0:T(8,128)S(1)}, u32[]{:S(2)}, u32[]{:S(2)}) %collective-permute-start.2) | collective-permute-done | bytes 16416 | tf_op jit(solution)/shard_map/ppermute | solution.py:308
  71.6 2.3 %collective-permute-start.3 = (f32[32,256]{1,0:T(8,128)S(1)}, f32[32,256]{1,0:T(8,128)S(1)}, u32[]{:S(2)}, u32[]{:S(2)}) collective-permute-start(f32[32,256]{1,0:T(8,128)S(1)} %pad_maximum_fusion), channel_id=1, source_target_pairs={{0,8},{1,9},{2,10},{3,11},{4,12},{5,13},{6,14},{7,15},{8,0},{9,1},... | collective-permute-start | bytes 98312 | tf_op jit(solution)/shard_map/ppermute | solution.py:308
  74.0 2.6 %collective-permute-done.3 = f32[32,256]{1,0:T(8,128)S(1)} collective-permute-done((f32[32,256]{1,0:T(8,128)S(1)}, f32[32,256]{1,0:T(8,128)S(1)}, u32[]{:S(2)}, u32[]{:S(2)}) %collective-permute-start.3) | collective-permute-done | bytes 32800 | tf_op jit(solution)/shard_map/ppermute | solution.py:308
  76.5 2.4 %concatenate.42.all_ref = f32[64,256]{1,0:T(8,128)} concatenate(f32[4,256]{1,0:T(4,128)S(1)} %copy-done.1, f32[4,256]{1,0:T(4,128)S(1)} %collective-permute-done, f32[8,256]{1,0:T(8,128)S(1)} %collective-permute-done.1, f32[16,256]{1,0:T(8,128)S(1)} %collective-permute-done.2, f32[32,256]{1,0:T(8,128)S(1)} %collective-permute-done.3), dimensions={0} | concatenate | bytes 131072 | tf_op jit(solution)/shard_map/concatenate | solution.py:343
  79.1 12.6 %shard_map.59 = (f32[4,256]{1,0:T(4,128)}, f32[256,256]{1,0:T(8,128)}, f32[256,256]{1,0:T(8,128)}) custom-call(f32[64,256]{1,0:T(8,128)} %concatenate.42.all_ref, f32[4,256]{1,0:T(4,128)} %get-tuple-element.12.own_ref, f32[256,256]{1,0:T(8,128)} %get-tuple-element.13.gram_c_ref), custom_call_target="tpu_custom_call" | custom-call | flops 10000000000 | bytes 1000000 | tf_op jit(solution)/shard_map/pallas_call | solution.py:211
  92.8 13.4 %shard_map.60 = (f32[1152,256]{1,0:T(8,128)}, f32[1,256]{1,0:T(1,128)}, f32[256,256]{1,0:T(8,128)}, f32[16,40,256]{2,1,0:T(8,128)}) custom-call(f32[4,576,1152]{2,1,0:T(8,128)} %bitcast.54, f32[4,256]{1,0:T(4,128)} %get-tuple-element.9.a_ref, f32[256,1152]{1,0:T(8,128)} %bitcast.41, f32[256,256]{1,0:T(8,128)} %get-tuple-element.16.inv_ref), custom_call_target="tpu_custom_call" | custom-call | flops 4076863488 | bytes 10616832 | tf_op jit(solution)/shard_map/pallas_call | solution.py:260
  110.1 1.6 %collective-permute-start.13 = (f32[4,40,256]{2,1,0:T(8,128)S(1)}, f32[4,40,256]{2,1,0:T(8,128)S(1)}, u32[]{:S(2)}, u32[]{:S(2)}) collective-permute-start(f32[4,40,256]{2,1,0:T(8,128)S(1)} %dynamic-slice_bitcast_fusion.3), channel_id=1, source_target_pairs={{0,2},{1,3},{2,0},{3,1},{4,6},{5,7},{6,4},{7,5},{8,10},{9,11},{10,... | collective-permute-start | bytes 491528 | tf_op jit(solution)/shard_map/ppermute | solution.py:308
  111.7 4.9 %collective-permute-done.13 = f32[4,40,256]{2,1,0:T(8,128)S(1)} collective-permute-done((f32[4,40,256]{2,1,0:T(8,128)S(1)}, f32[4,40,256]{2,1,0:T(8,128)S(1)}, u32[]{:S(2)}, u32[]{:S(2)}) %collective-permute-start.13) | collective-permute-done | bytes 163872 | tf_op jit(solution)/shard_map/ppermute | solution.py:308
  116.7 2.1 %collective-permute-start.14 = (f32[2,40,256]{2,1,0:T(8,128)S(1)}, f32[2,40,256]{2,1,0:T(8,128)S(1)}, u32[]{:S(2)}, u32[]{:S(2)}) collective-permute-start(f32[2,40,256]{2,1,0:T(8,128)S(1)} %dynamic-slice_bitcast_fusion.5), channel_id=1, source_target_pairs={{0,4},{1,5},{2,6},{3,7},{4,0},{5,1},{6,2},{7,3},{8,12},{9,13},{10,... | collective-permute-start | bytes 245768 | tf_op jit(solution)/shard_map/ppermute | solution.py:308
  118.8 2.4 %collective-permute-done.14 = f32[2,40,256]{2,1,0:T(8,128)S(1)} collective-permute-done((f32[2,40,256]{2,1,0:T(8,128)S(1)}, f32[2,40,256]{2,1,0:T(8,128)S(1)}, u32[]{:S(2)}, u32[]{:S(2)}) %collective-permute-start.14) | collective-permute-done | bytes 81952 | tf_op jit(solution)/shard_map/ppermute | solution.py:308
  121.2 2.3 %collective-permute-start.15 = (f32[1,40,256]{2,1,0:T(8,128)S(1)}, f32[1,40,256]{2,1,0:T(8,128)S(1)}, u32[]{:S(2)}, u32[]{:S(2)}) collective-permute-start(f32[1,40,256]{2,1,0:T(8,128)S(1)} %constant_dynamic-slice_fusion), channel_id=1, source_target_pairs={{0,8},{1,9},{2,10},{3,11},{4,12},{5,13},{6,14},{7,15},{8,0},{9,1},... | collective-permute-start | bytes 122888 | tf_op jit(solution)/shard_map/ppermute | solution.py:308
  123.5 12.1 %shard_map.61 = f32[256,256]{1,0:T(8,128)} custom-call(f32[256,256]{1,0:T(8,128)} %get-tuple-element.19.a_ref, f32[256,256]{1,0:T(8,128)} %get-tuple-element.20.b_ref), custom_call_target="tpu_custom_call" | custom-call | flops 10000000000 | bytes 1000000 | tf_op jit(solution)/shard_map/pallas_call | solution.py:298
  138.0 1.5 %collective-permute-start.17 = (f32[1,256]{1,0:T(1,128)S(1)}, f32[1,256]{1,0:T(1,128)S(1)}, u32[]{:S(2)}, u32[]{:S(2)}) collective-permute-start(f32[1,256]{1,0:T(1,128)S(1)} %add.106), channel_id=1, source_target_pairs={{0,2},{1,3},{2,0},{3,1},{4,6},{5,7},{6,4},{7,5},{8,10},{9,11},{10,... | collective-permute-start | bytes 3080 | tf_op jit(solution)/shard_map/ppermute | solution.py:308
  139.6 2.0 %collective-permute-done.17 = f32[1,256]{1,0:T(1,128)S(1)} collective-permute-done((f32[1,256]{1,0:T(1,128)S(1)}, f32[1,256]{1,0:T(1,128)S(1)}, u32[]{:S(2)}, u32[]{:S(2)}) %collective-permute-start.17) | collective-permute-done | bytes 1056 | tf_op jit(solution)/shard_map/ppermute | solution.py:308
  141.6 2.0 %collective-permute-start.18 = (f32[1,256]{1,0:T(1,128)S(1)}, f32[1,256]{1,0:T(1,128)S(1)}, u32[]{:S(2)}, u32[]{:S(2)}) collective-permute-start(f32[1,256]{1,0:T(1,128)S(1)} %add.107), channel_id=1, source_target_pairs={{0,4},{1,5},{2,6},{3,7},{4,0},{5,1},{6,2},{7,3},{8,12},{9,13},{10,... | collective-permute-start | bytes 3080 | tf_op jit(solution)/shard_map/ppermute | solution.py:308
  143.6 1.6 %collective-permute-done.18 = f32[1,256]{1,0:T(1,128)S(1)} collective-permute-done((f32[1,256]{1,0:T(1,128)S(1)}, f32[1,256]{1,0:T(1,128)S(1)}, u32[]{:S(2)}, u32[]{:S(2)}) %collective-permute-start.18) | collective-permute-done | bytes 1056 | tf_op jit(solution)/shard_map/ppermute | solution.py:308
  147.4 2.3 %collective-permute-done.19 = f32[1,256]{1,0:T(1,128)S(1)} collective-permute-done((f32[1,256]{1,0:T(1,128)S(1)}, f32[1,256]{1,0:T(1,128)S(1)}, u32[]{:S(2)}, u32[]{:S(2)}) %collective-permute-start.19) | collective-permute-done | bytes 1056 | tf_op jit(solution)/shard_map/ppermute | solution.py:308
  (47 shorter events, 12.9 us)
Async XLA Ops:
  24.3 3.4 %copy-start = (f32[256,1152]{1,0:T(8,128)S(1)}, f32[256,1152]{1,0:T(8,128)}, u32[]{:S(2)}) copy-start(f32[256,1152]{1,0:T(8,128)} %get-tuple-element.15) | copy-start | bytes 3538948
  25.5 2.1 %collective-permute-start.4 = (f32[8,16,1152]{2,1,0:T(8,128)S(1)}, f32[8,16,1152]{2,1,0:T(8,128)S(1)}, u32[]{:S(2)}, u32[]{:S(2)}) collective-permute-start(f32[8,16,1152]{2,1,0:T(8,128)S(1)} %dynamic-slice_bitcast_fusion), channel_id=1, source_target_pairs={{0,1},{1,0},{2,3},{3,2},{4,5},{5,4},{6,7},{7,6},{8,9},{9,8},{10,11... | collective-permute-start | bytes 1769480 | tf_op jit(solution)/shard_map/ppermute | solution.py:308
  27.7 30.0 %copy-start.1 = (f32[4,256]{1,0:T(4,128)S(1)}, f32[4,256]{1,0:T(4,128)}, u32[]{:S(2)}) copy-start(f32[4,256]{1,0:T(4,128)} %get-tuple-element.12.own_ref) | copy-start | bytes 12292
  27.8 10.3 %collective-permute-start.5 = (f32[4,16,1152]{2,1,0:T(8,128)S(1)}, f32[4,16,1152]{2,1,0:T(8,128)S(1)}, u32[]{:S(2)}, u32[]{:S(2)}) collective-permute-start(f32[4,16,1152]{2,1,0:T(8,128)S(1)} %dynamic-slice_bitcast_fusion.2), channel_id=1, source_target_pairs={{0,2},{1,3},{2,0},{3,1},{4,6},{5,7},{6,4},{7,5},{8,10},{9,11},{10,... | collective-permute-start | bytes 884744 | tf_op jit(solution)/shard_map/ppermute | solution.py:308
  38.1 5.4 %collective-permute-start.6 = (f32[2,16,1152]{2,1,0:T(8,128)S(1)}, f32[2,16,1152]{2,1,0:T(8,128)S(1)}, u32[]{:S(2)}, u32[]{:S(2)}) collective-permute-start(f32[2,16,1152]{2,1,0:T(8,128)S(1)} %dynamic-slice_bitcast_fusion.4), channel_id=1, source_target_pairs={{0,4},{1,5},{2,6},{3,7},{4,0},{5,1},{6,2},{7,3},{8,12},{9,13},{10,... | collective-permute-start | bytes 442376 | tf_op jit(solution)/shard_map/ppermute | solution.py:308
  43.6 5.3 %collective-permute-start.7 = (f32[1,16,1152]{2,1,0:T(8,128)S(1)}, f32[1,16,1152]{2,1,0:T(8,128)S(1)}, u32[]{:S(2)}, u32[]{:S(2)}) collective-permute-start(f32[1,16,1152]{2,1,0:T(8,128)S(1)} %constant_dynamic-slice_fusion.2), channel_id=1, source_target_pairs={{0,8},{1,9},{2,10},{3,11},{4,12},{5,13},{6,14},{7,15},{8,0},{9,1},... | collective-permute-start | bytes 221192 | tf_op jit(solution)/shard_map/ppermute | solution.py:308
  48.9 5.3 %collective-permute-start.8 = (f32[1,16,1152]{2,1,0:T(8,128)S(1)}, f32[1,16,1152]{2,1,0:T(8,128)S(1)}, u32[]{:S(2)}, u32[]{:S(2)}) collective-permute-start(f32[1,16,1152]{2,1,0:T(8,128)S(1)} %dynamic-slice_add_fusion), channel_id=1, source_target_pairs={{0,8},{1,9},{2,10},{3,11},{4,12},{5,13},{6,14},{7,15},{8,0},{9,1},... | collective-permute-start | bytes 221192 | tf_op jit(solution)/shard_map/ppermute | solution.py:308
  54.3 6.6 %collective-permute-start.9 = (f32[2,16,1152]{2,1,0:T(8,128)S(1)}, f32[2,16,1152]{2,1,0:T(8,128)S(1)}, u32[]{:S(2)}, u32[]{:S(2)}) collective-permute-start(f32[2,16,1152]{2,1,0:T(8,128)S(1)} %maximum_select_fusion.3), channel_id=1, source_target_pairs={{0,4},{1,5},{2,6},{3,7},{4,0},{5,1},{6,2},{7,3},{8,12},{9,13},{10,... | collective-permute-start | bytes 442376 | tf_op jit(solution)/shard_map/ppermute | solution.py:308
  57.8 4.7 %collective-permute-start = (f32[4,256]{1,0:T(4,128)S(1)}, f32[4,256]{1,0:T(4,128)S(1)}, u32[]{:S(2)}, u32[]{:S(2)}) collective-permute-start(f32[4,256]{1,0:T(4,128)S(1)} %copy-done.1), channel_id=1, source_target_pairs={{0,1},{1,0},{2,3},{3,2},{4,5},{5,4},{6,7},{7,6},{8,9},{9,8},{10,11... | collective-permute-start | bytes 12296 | tf_op jit(solution)/shard_map/ppermute | solution.py:308
  60.9 18.0 %collective-permute-start.10 = (f32[4,16,1152]{2,1,0:T(8,128)S(1)}, f32[4,16,1152]{2,1,0:T(8,128)S(1)}, u32[]{:S(2)}, u32[]{:S(2)}) collective-permute-start(f32[4,16,1152]{2,1,0:T(8,128)S(1)} %maximum_select_fusion.2), channel_id=1, source_target_pairs={{0,2},{1,3},{2,0},{3,1},{4,6},{5,7},{6,4},{7,5},{8,10},{9,11},{10,... | collective-permute-start | bytes 884744 | tf_op jit(solution)/shard_map/ppermute | solution.py:308
  62.5 5.3 %collective-permute-start.1 = (f32[8,256]{1,0:T(8,128)S(1)}, f32[8,256]{1,0:T(8,128)S(1)}, u32[]{:S(2)}, u32[]{:S(2)}) collective-permute-start(f32[8,256]{1,0:T(8,128)S(1)} %pad_maximum_fusion.2), channel_id=1, source_target_pairs={{0,2},{1,3},{2,0},{3,1},{4,6},{5,7},{6,4},{7,5},{8,10},{9,11},{10,... | collective-permute-start | bytes 24584 | tf_op jit(solution)/shard_map/ppermute | solution.py:308
  67.8 3.8 %collective-permute-start.2 = (f32[16,256]{1,0:T(8,128)S(1)}, f32[16,256]{1,0:T(8,128)S(1)}, u32[]{:S(2)}, u32[]{:S(2)}) collective-permute-start(f32[16,256]{1,0:T(8,128)S(1)} %pad_maximum_fusion.1), channel_id=1, source_target_pairs={{0,4},{1,5},{2,6},{3,7},{4,0},{5,1},{6,2},{7,3},{8,12},{9,13},{10,... | collective-permute-start | bytes 49160 | tf_op jit(solution)/shard_map/ppermute | solution.py:308
  71.6 4.9 %collective-permute-start.3 = (f32[32,256]{1,0:T(8,128)S(1)}, f32[32,256]{1,0:T(8,128)S(1)}, u32[]{:S(2)}, u32[]{:S(2)}) collective-permute-start(f32[32,256]{1,0:T(8,128)S(1)} %pad_maximum_fusion), channel_id=1, source_target_pairs={{0,8},{1,9},{2,10},{3,11},{4,12},{5,13},{6,14},{7,15},{8,0},{9,1},... | collective-permute-start | bytes 98312 | tf_op jit(solution)/shard_map/ppermute | solution.py:308
  79.0 12.6 %collective-permute-start.11 = (f32[8,16,1152]{2,1,0:T(8,128)S(1)}, f32[8,16,1152]{2,1,0:T(8,128)S(1)}, u32[]{:S(2)}, u32[]{:S(2)}) collective-permute-start(f32[8,16,1152]{2,1,0:T(8,128)S(1)} %maximum_select_fusion.1), channel_id=1, source_target_pairs={{0,1},{1,0},{2,3},{3,2},{4,5},{5,4},{6,7},{7,6},{8,9},{9,8},{10,11... | collective-permute-start | bytes 1769480 | tf_op jit(solution)/shard_map/ppermute | solution.py:308
  107.2 1.8 %collective-permute-start.12 = (f32[8,40,256]{2,1,0:T(8,128)S(1)}, f32[8,40,256]{2,1,0:T(8,128)S(1)}, u32[]{:S(2)}, u32[]{:S(2)}) collective-permute-start(f32[8,40,256]{2,1,0:T(8,128)S(1)} %dynamic-slice_bitcast_fusion.1), channel_id=1, source_target_pairs={{0,1},{1,0},{2,3},{3,2},{4,5},{5,4},{6,7},{7,6},{8,9},{9,8},{10,11... | collective-permute-start | bytes 983048 | tf_op jit(solution)/shard_map/ppermute | solution.py:308
  110.1 6.5 %collective-permute-start.13 = (f32[4,40,256]{2,1,0:T(8,128)S(1)}, f32[4,40,256]{2,1,0:T(8,128)S(1)}, u32[]{:S(2)}, u32[]{:S(2)}) collective-permute-start(f32[4,40,256]{2,1,0:T(8,128)S(1)} %dynamic-slice_bitcast_fusion.3), channel_id=1, source_target_pairs={{0,2},{1,3},{2,0},{3,1},{4,6},{5,7},{6,4},{7,5},{8,10},{9,11},{10,... | collective-permute-start | bytes 491528 | tf_op jit(solution)/shard_map/ppermute | solution.py:308
  116.7 4.5 %collective-permute-start.14 = (f32[2,40,256]{2,1,0:T(8,128)S(1)}, f32[2,40,256]{2,1,0:T(8,128)S(1)}, u32[]{:S(2)}, u32[]{:S(2)}) collective-permute-start(f32[2,40,256]{2,1,0:T(8,128)S(1)} %dynamic-slice_bitcast_fusion.5), channel_id=1, source_target_pairs={{0,4},{1,5},{2,6},{3,7},{4,0},{5,1},{6,2},{7,3},{8,12},{9,13},{10,... | collective-permute-start | bytes 245768 | tf_op jit(solution)/shard_map/ppermute | solution.py:308
  121.2 14.4 %collective-permute-start.15 = (f32[1,40,256]{2,1,0:T(8,128)S(1)}, f32[1,40,256]{2,1,0:T(8,128)S(1)}, u32[]{:S(2)}, u32[]{:S(2)}) collective-permute-start(f32[1,40,256]{2,1,0:T(8,128)S(1)} %constant_dynamic-slice_fusion), channel_id=1, source_target_pairs={{0,8},{1,9},{2,10},{3,11},{4,12},{5,13},{6,14},{7,15},{8,0},{9,1},... | collective-permute-start | bytes 122888 | tf_op jit(solution)/shard_map/ppermute | solution.py:308
  136.8 1.2 collective-permute-start.16
  138.0 3.6 %collective-permute-start.17 = (f32[1,256]{1,0:T(1,128)S(1)}, f32[1,256]{1,0:T(1,128)S(1)}, u32[]{:S(2)}, u32[]{:S(2)}) collective-permute-start(f32[1,256]{1,0:T(1,128)S(1)} %add.106), channel_id=1, source_target_pairs={{0,2},{1,3},{2,0},{3,1},{4,6},{5,7},{6,4},{7,5},{8,10},{9,11},{10,... | collective-permute-start | bytes 3080 | tf_op jit(solution)/shard_map/ppermute | solution.py:308
  141.6 3.6 %collective-permute-start.18 = (f32[1,256]{1,0:T(1,128)S(1)}, f32[1,256]{1,0:T(1,128)S(1)}, u32[]{:S(2)}, u32[]{:S(2)}) collective-permute-start(f32[1,256]{1,0:T(1,128)S(1)} %add.107), channel_id=1, source_target_pairs={{0,4},{1,5},{2,6},{3,7},{4,0},{5,1},{6,2},{7,3},{8,12},{9,13},{10,... | collective-permute-start | bytes 3080 | tf_op jit(solution)/shard_map/ppermute | solution.py:308
  145.2 4.5 %collective-permute-start.19 = (f32[1,256]{1,0:T(1,128)S(1)}, f32[1,256]{1,0:T(1,128)S(1)}, u32[]{:S(2)}, u32[]{:S(2)}) collective-permute-start(f32[1,256]{1,0:T(1,128)S(1)} %add.108), channel_id=1, source_target_pairs={{0,8},{1,9},{2,10},{3,11},{4,12},{5,13},{6,14},{7,15},{8,0},{9,1},... | collective-permute-start | bytes 3080 | tf_op jit(solution)/shard_map/ppermute | solution.py:308

commit v2 on v1

--- a/solution.py
+++ b/solution.py
@@ -244,9 +244,8 @@
         result = total[...] * new_ref[...]
         devices, padded, _ = out_ref.shape
         rows = result.shape[0] // devices
-        steps = devices.bit_length() - 1
         for d in range(devices):
-            place = sum(((d >> b) & 1) << (steps - 1 - b) for b in range(steps))
+            place = (d % 2) * (devices // 2) + d // 2
             out_ref[place, :rows, :] = result[d * rows : (d + 1) * rows, :]
             if padded > rows:
                 out_ref[place, rows:, :] = jnp.zeros((padded - rows, result.shape[1]), jnp.float32)
@@ -308,52 +307,54 @@
     return lax.ppermute(x, "gx", [(i, i ^ (1 << bit)) for i in range(devices)])
 
 
-def scatter(x, steps):
-    me = lax.axis_index("gx")
-    for bit in range(steps):
-        mine = (me >> bit) & 1
-        half = x.shape[0] // 2
-        x = x.reshape((2, half) + x.shape[1:])
-        keep = lax.dynamic_index_in_dim(x, mine, 0, keepdims=False)
-        send = lax.dynamic_index_in_dim(x, 1 - mine, 0, keepdims=False)
-        x = keep + swap(send, bit)
-    return x
-
-
-def gather(x, steps):
-    me = lax.axis_index("gx")
-    for bit in reversed(range(steps)):
-        mine = (me >> bit) & 1
-        other = swap(x, bit)
-        x = jnp.where(
-            mine == 0, jnp.concatenate([x, other], axis=0), jnp.concatenate([other, x], axis=0)
-        )
-    return x
+def exchange(x, groups):
+    return lax.all_to_all(x, "gx", 0, 0, axis_index_groups=groups, tiled=True)
+
+
+def chips():
+    devices = lax.axis_size("gx")
+    return [[2 * chip + core for chip in range(devices // 2)] for core in range(2)]
+
+
+def scatter(x):
+    core = lax.axis_index("gx") & 1
+    keep = lax.dynamic_index_in_dim(x, core, 0, keepdims=False)
+    send = lax.dynamic_index_in_dim(x, 1 - core, 0, keepdims=False)
+    return jnp.sum(exchange(keep + swap(send, 0), chips()), axis=0)
+
+
+def gather(x):
+    core = lax.axis_index("gx") & 1
+    members = lax.axis_size("gx") // 2
+    x = exchange(jnp.broadcast_to(x[None], (members,) + x.shape), chips())
+    other = swap(x, 0)
+    return jnp.where(core == 0, jnp.stack([x, other]), jnp.stack([other, x]))
+
+
+def gather_small(x):
+    devices = lax.axis_size("gx")
+    x = exchange(jnp.broadcast_to(x[None], (devices,) + x.shape), None)
+    return x.reshape((-1,) + x.shape[2:])
 
 
 def local(tensor, factor_b, factor_c):
     devices = lax.axis_size("gx")
     me = lax.axis_index("gx")
-    steps = devices.bit_length() - 1
     total_second, total_third = tensor.shape[1], tensor.shape[2]
     turned = jnp.swapaxes(tensor, 1, 2)
     raw_a, side_b, gram_c = first_call(turned, factor_b, factor_c)
-    gathered = raw_a
-    for bit in range(steps):
-        gathered = jnp.concatenate([gathered, swap(gathered, bit)], axis=0)
     rank = raw_a.shape[1]
-    side_b = side_b.reshape(devices, rank // devices, total_second)
-    side_b = gather(scatter(side_b, steps), steps).reshape(rank, total_second)
+    gathered = gather_small(raw_a)
+    side_b = side_b.reshape(2, devices // 2, rank // devices, total_second)
+    side_b = gather(scatter(side_b)).reshape(rank, total_second)
     new_a, gram_a, inv_b = second_call(gathered, raw_a, gram_c)
     all_b, _, gram_b, side_c = third_call(turned, new_a, side_b, inv_b, devices)
     rows_b = total_second // devices
     new_b = lax.dynamic_slice_in_dim(all_b, me * rows_b, rows_b, axis=0)
     inv_c = fourth_call(gram_a, gram_b)
-    side_c = scatter(side_c, steps)[0]
+    side_c = scatter(side_c.reshape((2, devices // 2) + side_c.shape[1:]))
     raw_c = dot(side_c, inv_c)[: total_third // devices]
-    sums = jnp.sum(raw_c * raw_c, axis=0, keepdims=True)
-    for bit in range(steps):
-        sums = sums + swap(sums, bit)
+    sums = jnp.sum(gather_small(jnp.sum(raw_c * raw_c, axis=0, keepdims=True)), axis=0)
     new_c = raw_c * jnp.sqrt(total_third / (sums + 1e-06))
     return (new_a, new_b, new_c)
 

time: 151 us -> 146 us (0.967)
  blocking collectives: 0 us -> 23.8 us
  waiting for transfers between devices: 45.6 us -> 29.6 us
  starting transfers between devices: 31.7 us -> 18 us
    ppermute x20 -> x3, waiting for transfers between devices: 45.6 us -> 2.89 us  [swap(): return lax.ppermute(x, 'gx', [(i, i ^ 1 << bit) for i in range(devices)])]
    ppermute x20 -> x3, starting transfers between devices: 31.7 us -> 1.09 us  [swap(): return lax.ppermute(x, 'gx', [(i, i ^ 1 << bit) for i in range(devices)])]
    all_to_all x0 -> x4, waiting for transfers between devices: none -> 26.8 us  [exchange(): return lax.all_to_all(x, 'gx', 0, 0, axis_index_groups=groups, tiled=True)]
    all_to_all x0 -> x1, blocking collectives: none -> 23.8 us  [exchange(): return lax.all_to_all(x, 'gx', 0, 0, axis_index_groups=groups, tiled=True)]
    all_to_all x0 -> x4, starting transfers between devices: none -> 16.9 us  [exchange(): return lax.all_to_all(x, 'gx', 0, 0, axis_index_groups=groups, tiled=True)]
    concatenate x1 -> x0, local copies, waits for them, and re-layouts: 2.43 us -> none  [local(): gathered = jnp.concatenate([gathered, swap(gathered, bit)], axis=0)]
    broadcast_in_dim x0 -> x3, local copies, waits for them, and re-layouts: none -> 2.12 us  [the longest x2 1.26 us: gather_small(): x = exchange(jnp.broadcast_to(x[None], (devices,) + x.shape), None)]
  transfers between devices with their start and end apart: 20 -> 7, of which waited for: 16 -> 5; matrix products, arithmetic and copies ran while one was open for 3% -> 2% of each run, Pallas kernels for 16% -> 17%
where the time goes in v2:
time: 146 us; the launch traced here: 145 us
  Pallas kernels  61.7 us (42%)
  waiting for transfers between devices  29.6 us (20%)
  blocking collectives  23.8 us (16%)
  starting transfers between devices  18 us (12%)
  local copies, waits for them, and re-layouts  6.5 us (4%)
  other arithmetic  3.66 us (3%)
    all_to_all x4, waiting for transfers between devices, exchange(): return lax.all_to_all(x, 'gx', 0, 0, axis_index_groups=groups, tiled=True)  26.8 us
    all_to_all x1, blocking collectives, exchange(): return lax.all_to_all(x, 'gx', 0, 0, axis_index_groups=groups, tiled=True)  23.8 us
    pallas_call x1, Pallas kernels, first_call(): pl.pallas_call(first_kernel, grid=(count,), in_specs=[pl.BlockSpec((1, de...  23.7 us
    all_to_all x4, starting transfers between devices, exchange(): return lax.all_to_all(x, 'gx', 0, 0, axis_index_groups=groups, tiled=True)  16.9 us
    pallas_call x1, Pallas kernels, third_call(): pl.pallas_call(third_kernel, grid=(count,), in_specs=[pl.BlockSpec((1, de...  13.4 us
    pallas_call x1, Pallas kernels, second_call(): pl.pallas_call(functools.partial(second_kernel, float(gathered.shape[0]))...  12.6 us
    pallas_call x1, Pallas kernels, fourth_call(): pl.pallas_call(fourth_kernel, out_shape=jax.ShapeDtypeStruct(gram_a.shape...  12.1 us
  transfers between devices with their start and end apart: 7, of which 5 were waited for; matrix products, arithmetic and copies ran while one was open for 2% of the time, Pallas kernels for 17%

profile of v2, /device:TPU:0, one launch (start us, length us, event | category | flops | bytes accessed | tf_op | source)
XLA Modules:
  0.0 145.3 jit_solution(6875094875751552061)
XLA Ops:
  0.6 23.7 %shard_map.58 = (f32[4,256]{1,0:T(4,128)}, f32[256,1152]{1,0:T(8,128)}, f32[256,256]{1,0:T(8,128)}) custom-call(f32[4,576,1152]{2,1,0:T(8,128)} %bitcast.22, f32[1152,256]{1,0:T(8,128)} %b_ref.1, f32[576,256]{1,0:T(8,128)} %c_ref.1), custom_call_target="tpu_custom_call" | custom-call | flops 4076863488 | bytes 10616832 | tf_op jit(solution)/shard_map/pallas_call | solution.py:157
  24.3 1.2 dynamic-slice_bitcast_fusion
  25.5 0.5 collective-permute-start
  26.0 1.6 %collective-permute-done = f32[8,16,1152]{2,1,0:T(8,128)S(1)} collective-permute-done((f32[8,16,1152]{2,1,0:T(8,128)S(1)}, f32[8,16,1152]{2,1,0:T(8,128)S(1)}, u32[]{:S(2)}, u32[]{:S(2)}) %collective-permute-start) | collective-permute-done | bytes 589856 | tf_op jit(solution)/shard_map/ppermute | solution.py:307
  27.6 0.0 copy-done
  27.6 0.1 bitcast_add_fusion
  27.7 23.8 %all_to_all.25 = f32[8,16,1152]{2,1,0:T(8,128)S(1)} all-to-all(f32[8,16,1152]{2,1,0:T(8,128)S(1)} %bitcast_add_fusion), channel_id=1, replica_groups={{0,2,4,6,8,10,12,14},{1,3,5,7,9,11,13,15},{16,18,20,22,24,26,28,30},{17..., dimensions={0} | all-to-all | bytes 1179648 | tf_op jit(solution)/shard_map/all_to_all | solution.py:311
  51.5 0.6 broadcast_in_dim.6
  52.2 3.5 %all-to-all-start = ((f32[16,4,256]{2,1,0:T(4,128)}), f32[16,4,256]{2,1,0:T(4,128)S(1)}, u32[]{:S(2)}, u32[]{:S(2)}) async-start(f32[16,4,256]{2,1,0:T(4,128)} %broadcast_in_dim.6), calls=%async_computation | async-start | bytes 131072 | tf_op jit(solution)/shard_map/all_to_all | solution.py:311
  55.7 6.8 %all-to-all-done = f32[16,4,256]{2,1,0:T(4,128)S(1)} async-done(((f32[16,4,256]{2,1,0:T(4,128)}), f32[16,4,256]{2,1,0:T(4,128)S(1)}, u32[]{:S(2)}, u32[]{:S(2)}) %all-to-all-start) | async-done | bytes 65568 | tf_op jit(solution)/shard_map/all_to_all | solution.py:311
  62.6 0.9 broadcast_in_dim.7
  63.4 3.7 %all-to-all-start.2 = ((f32[8,16,1152]{2,1,0:T(8,128)}), f32[8,16,1152]{2,1,0:T(8,128)S(1)}, u32[]{:S(2)}, u32[]{:S(2)}) async-start(f32[8,16,1152]{2,1,0:T(8,128)} %broadcast_in_dim.7), calls=%async_computation.2 | async-start | bytes 1179648 | tf_op jit(solution)/shard_map/all_to_all | solution.py:311
  67.1 0.7 reshape.31.all_ref
  67.8 15.0 %all-to-all-done.2 = f32[8,16,1152]{2,1,0:T(8,128)S(1)} async-done(((f32[8,16,1152]{2,1,0:T(8,128)}), f32[8,16,1152]{2,1,0:T(8,128)S(1)}, u32[]{:S(2)}, u32[]{:S(2)}) %all-to-all-start.2) | async-done | bytes 589856 | tf_op jit(solution)/shard_map/all_to_all | solution.py:311
  82.8 0.0 collective-permute-start.1
  82.8 12.6 %shard_map.59 = (f32[4,256]{1,0:T(4,128)}, f32[256,256]{1,0:T(8,128)}, f32[256,256]{1,0:T(8,128)}) custom-call(f32[64,256]{1,0:T(8,128)} %reshape.31.all_ref, f32[4,256]{1,0:T(4,128)} %get-tuple-element.12.own_ref, f32[256,256]{1,0:T(8,128)} %get-tuple-element.13.gram_c_ref), custom_call_target="tpu_custom_call" | custom-call | flops 10000000000 | bytes 1000000 | tf_op jit(solution)/shard_map/pallas_call | solution.py:211
  95.3 0.0 collective-permute-done.1
  95.3 1.1 maximum_select_fusion
  96.5 13.4 %shard_map.60 = (f32[1152,256]{1,0:T(8,128)}, f32[1,256]{1,0:T(1,128)}, f32[256,256]{1,0:T(8,128)}, f32[16,40,256]{2,1,0:T(8,128)}) custom-call(f32[4,576,1152]{2,1,0:T(8,128)} %bitcast.23, f32[4,256]{1,0:T(4,128)} %get-tuple-element.9.a_ref, f32[256,1152]{1,0:T(8,128)} %bitcast.16, f32[256,256]{1,0:T(8,128)} %get-tuple-element.16.inv_ref), custom_call_target="tpu_custom_call" | custom-call | flops 4076863488 | bytes 10616832 | tf_op jit(solution)/shard_map/pallas_call | solution.py:259
  109.9 1.0 dynamic-slice_bitcast_fusion.1
  110.9 0.6 collective-permute-start.2
  111.5 1.3 collective-permute-done.2
  112.7 1.8 %bitcast_add_fusion.1 = f32[8,40,256]{2,1,0:T(8,128)} fusion(f32[8,40,256]{2,1,0:T(8,128)S(1)} %collective-permute-done.2, f32[2,8,40,256]{3,2,1,0:T(8,128)} %bitcast.20, s32[]{:T(128)S(6)} %select_n.26), kind=kLoop, calls=%fused_computation.3 | loop fusion | flops 81920 | bytes 983044 | tf_op jit(solution)/shard_map/add | solution.py:323
  114.5 3.7 %all-to-all-start.3 = ((f32[8,40,256]{2,1,0:T(8,128)}), f32[8,40,256]{2,1,0:T(8,128)S(1)}, u32[]{:S(2)}, u32[]{:S(2)}) async-start(f32[8,40,256]{2,1,0:T(8,128)} %bitcast_add_fusion.1), calls=%async_computation.3 | async-start | bytes 655360 | tf_op jit(solution)/shard_map/all_to_all | solution.py:311
  118.1 12.1 %shard_map.61 = f32[256,256]{1,0:T(8,128)} custom-call(f32[256,256]{1,0:T(8,128)} %get-tuple-element.19.a_ref, f32[256,256]{1,0:T(8,128)} %get-tuple-element.20.b_ref), custom_call_target="tpu_custom_call" | custom-call | flops 10000000000 | bytes 1000000 | tf_op jit(solution)/shard_map/pallas_call | solution.py:297
  130.2 0.0 all-to-all-done.3
  130.2 1.2 multiply_reduce_fusion
  131.4 0.6 broadcast_in_dim.8
  132.1 6.1 %all-to-all-start.4 = ((f32[16,1,256]{2,1,0:T(1,128)}), f32[16,1,256]{2,1,0:T(1,128)S(1)}, u32[]{:S(2)}, u32[]{:S(2)}) async-start(f32[16,1,256]{2,1,0:T(1,128)} %broadcast_in_dim.8), calls=%async_computation.4 | async-start | bytes 32768 | tf_op jit(solution)/shard_map/all_to_all | solution.py:311
  138.1 1.5 %constant_dynamic-slice_fusion = f32[72,256]{1,0:T(8,128)} fusion(f32[1152,256]{1,0:T(8,128)} %get-tuple-element.17, s32[]{:T(128)S(6)} %select_n.30), kind=kLoop, calls=%fused_computation.9 | loop fusion | bytes 147460 | tf_op jit(solution)/shard_map/dynamic_slice | solution.py:353
  139.7 5.0 %all-to-all-done.4 = f32[16,1,256]{2,1,0:T(1,128)S(1)} async-done(((f32[16,1,256]{2,1,0:T(1,128)}), f32[16,1,256]{2,1,0:T(1,128)S(1)}, u32[]{:S(2)}, u32[]{:S(2)}) %all-to-all-start.4) | async-done | bytes 16416 | tf_op jit(solution)/shard_map/all_to_all | solution.py:311
  144.7 0.6 broadcast_multiply_fusion
  (7 shorter events, 0.1 us)
Async XLA Ops:
  24.3 3.4 %copy-start = (f32[256,1152]{1,0:T(8,128)S(1)}, f32[256,1152]{1,0:T(8,128)}, u32[]{:S(2)}) copy-start(f32[256,1152]{1,0:T(8,128)} %get-tuple-element.15) | copy-start | bytes 3538948
  25.5 2.1 %collective-permute-start = (f32[8,16,1152]{2,1,0:T(8,128)S(1)}, f32[8,16,1152]{2,1,0:T(8,128)S(1)}, u32[]{:S(2)}, u32[]{:S(2)}) collective-permute-start(f32[8,16,1152]{2,1,0:T(8,128)S(1)} %dynamic-slice_bitcast_fusion), channel_id=1, source_target_pairs={{0,1},{1,0},{2,3},{3,2},{4,5},{5,4},{6,7},{7,6},{8,9},{9,8},{10,11... | collective-permute-start | bytes 1769480 | tf_op jit(solution)/shard_map/ppermute | solution.py:307
  26.0 25.5 %copy-start.1 = (f32[4,256]{1,0:T(4,128)S(1)}, f32[4,256]{1,0:T(4,128)}, u32[]{:S(2)}) copy-start(f32[4,256]{1,0:T(4,128)} %get-tuple-element.12.own_ref) | copy-start | bytes 12292
  52.2 10.4 %all-to-all-start = ((f32[16,4,256]{2,1,0:T(4,128)}), f32[16,4,256]{2,1,0:T(4,128)S(1)}, u32[]{:S(2)}, u32[]{:S(2)}) async-start(f32[16,4,256]{2,1,0:T(4,128)} %broadcast_in_dim.6), calls=%async_computation | async-start | bytes 131072 | tf_op jit(solution)/shard_map/all_to_all | solution.py:311
  63.4 19.4 %all-to-all-start.2 = ((f32[8,16,1152]{2,1,0:T(8,128)}), f32[8,16,1152]{2,1,0:T(8,128)S(1)}, u32[]{:S(2)}, u32[]{:S(2)}) async-start(f32[8,16,1152]{2,1,0:T(8,128)} %broadcast_in_dim.7), calls=%async_computation.2 | async-start | bytes 1179648 | tf_op jit(solution)/shard_map/all_to_all | solution.py:311
  82.8 12.6 %collective-permute-start.1 = (f32[8,16,1152]{2,1,0:T(8,128)S(1)}, f32[8,16,1152]{2,1,0:T(8,128)S(1)}, u32[]{:S(2)}, u32[]{:S(2)}) collective-permute-start(f32[8,16,1152]{2,1,0:T(8,128)S(1)} %all-to-all-done.2), channel_id=1, source_target_pairs={{0,1},{1,0},{2,3},{3,2},{4,5},{5,4},{6,7},{7,6},{8,9},{9,8},{10,11... | collective-permute-start | bytes 1769480 | tf_op jit(solution)/shard_map/ppermute | solution.py:307
  110.9 1.8 %collective-permute-start.2 = (f32[8,40,256]{2,1,0:T(8,128)S(1)}, f32[8,40,256]{2,1,0:T(8,128)S(1)}, u32[]{:S(2)}, u32[]{:S(2)}) collective-permute-start(f32[8,40,256]{2,1,0:T(8,128)S(1)} %dynamic-slice_bitcast_fusion.1), channel_id=1, source_target_pairs={{0,1},{1,0},{2,3},{3,2},{4,5},{5,4},{6,7},{7,6},{8,9},{9,8},{10,11... | collective-permute-start | bytes 983048 | tf_op jit(solution)/shard_map/ppermute | solution.py:307
  114.5 15.7 %all-to-all-start.3 = ((f32[8,40,256]{2,1,0:T(8,128)}), f32[8,40,256]{2,1,0:T(8,128)S(1)}, u32[]{:S(2)}, u32[]{:S(2)}) async-start(f32[8,40,256]{2,1,0:T(8,128)} %bitcast_add_fusion.1), calls=%async_computation.3 | async-start | bytes 655360 | tf_op jit(solution)/shard_map/all_to_all | solution.py:311
  132.1 12.6 %all-to-all-start.4 = ((f32[16,1,256]{2,1,0:T(1,128)}), f32[16,1,256]{2,1,0:T(1,128)S(1)}, u32[]{:S(2)}, u32[]{:S(2)}) async-start(f32[16,1,256]{2,1,0:T(1,128)} %broadcast_in_dim.8), calls=%async_computation.4 | async-start | bytes 32768 | tf_op jit(solution)/shard_map/all_to_all | solution.py:311
